TPU v7x, 32 devices: a whole 2x2x4 slice. The times are simulated.
32 devices in a mesh: dp: 16 (over z, x, core), tensor: 2 (over y).
Axes of the slice: x: 2, y: 2, z: 4, core: 2. Of those that a mesh axis runs over, the one named last changes fastest.
Arguments:
- tokens: bfloat16 [6304, 768], P(('dp', 'tensor')), may hold values from -6 to 6
- w_qkv: bfloat16 [768, 3, 768], P('dp', None, 'tensor'), may hold values from -0.21875 to 0.21875
- w_mix: bfloat16 [768, 768], P('dp', 'tensor'), may hold values from -0.875 to 0.875
- w_router: bfloat16 [768, 16], P('dp'), may hold values from -0.15625 to 0.15625
- gain_one: bfloat16 [768], P('dp'), may hold values from 0.5 to 1.5
- shift_one: bfloat16 [768], P('dp'), may hold values from -1 to 1
- gain_two: bfloat16 [768], P('dp'), may hold values from 0.5 to 1.5
- shift_two: bfloat16 [768], P('dp'), may hold values from -1 to 1
- w_expand: bfloat16 [16, 768, 3072], P('dp', None, 'tensor'), may hold values from -0.21875 to 0.21875
- w_shrink: bfloat16 [16, 3072, 768], P('dp', 'tensor'), may hold values from -0.109375 to 0.109375
- expert_ids: int32 [6304, 2], P('dp'), may hold values from 0 to 15, as said below
- slot_ids: int32 [6304, 2], P('dp'), may hold values from 0 to 63, as said below
- keep_mask: int32 [6304, 2], P('dp'), may hold values from 0 to 1
- out_grad: bfloat16 [6304, 768], P(('dp', 'tensor')), may hold values from -6 to 6
Outputs:
- block_out: bfloat16 [6304, 768], P(('dp', 'tensor'))
- grad_tokens: float32 [6304, 768], P(('dp', 'tensor'))
- grad_w_qkv: float32 [768, 3, 768], P('dp', None, 'tensor')
- grad_w_mix: float32 [768, 768], P('dp', 'tensor')
- grad_router: float32 [768, 16], P(('dp', 'tensor'))
- grad_gain_one: float32 [768], P(('dp', 'tensor'))
- grad_shift_one: float32 [768], P(('dp', 'tensor'))
- grad_gain_two: float32 [768], P(('dp', 'tensor'))
- grad_shift_two: float32 [768], P(('dp', 'tensor'))
- grad_w_expand: float32 [16, 768, 3072], P('dp', None, 'tensor')
- grad_w_shrink: float32 [16, 3072, 768], P('dp', 'tensor')
Inputs may be any that keep to these rules, and one draw needn't show every extreme that they name: `expert_ids`: the two experts of a token differ. `slot_ids`: among the kept routes of the 394 rows of one index of dp, no two share an expert and a slot; a dropped route has slot 0.
All inputs are finite; a program needn't handle non-finite values.
Results may differ from a plain program's by a relative error of at most 0.017.
Values may be sent and summed in bfloat16 or wider, within the bound.
A program may use at most 128 MiB of HBM per device.

v0:
```python
import functools

import jax
import jax.numpy as jnp
from jax import lax
from jax.experimental import pallas as pl
from jax.experimental.pallas import tpu as pltpu
from jax.sharding import PartitionSpec as P

DH = 64
MESH = pl.DeviceIdType.MESH
VMEM = pl.BlockSpec(memory_space=pltpu.VMEM)
LIMIT = 48 * 1024 * 1024


def greet(peers):
    barrier = pltpu.get_barrier_semaphore()
    for peer in peers:
        pl.semaphore_signal(barrier, inc=1, device_id=peer, device_id_type=MESH)
    pl.semaphore_wait(barrier, len(peers))


def remote(src, dst, send, recv, peer):
    return pltpu.make_async_remote_copy(
        src_ref=src,
        dst_ref=dst,
        send_sem=send,
        recv_sem=recv,
        device_id=peer,
        device_id_type=MESH,
    )


def flip(me, mask):
    place = me
    bit = 1
    while bit <= mask:
        if mask & bit:
            place = place + bit - 2 * bit * lax.rem(me // bit, 2)
        bit *= 2
    return place


def low_bit(mask, n):
    return (mask & -mask) if mask else n


def bits_below(limit):
    bits = []
    bit = 1
    while bit < limit:
        bits.append(bit)
        bit *= 2
    return bits


def call(kernel, ident, outs, scratch, *operands):
    return pl.pallas_call(
        kernel,
        out_shape=outs,
        in_specs=[VMEM] * len(operands),
        out_specs=[VMEM] * len(outs),
        scratch_shapes=scratch,
        compiler_params=pltpu.CompilerParams(
            collective_id=ident, has_side_effects=True, vmem_limit_bytes=LIMIT
        ),
    )(*operands)


def shape_of(array):
    return jax.ShapeDtypeStruct(array.shape, array.dtype)


def swap_kernel(count, *refs):
    ins, outs = refs[:count], refs[count : 2 * count]
    send, recv = refs[2 * count :]
    other = {"tensor": 1 - lax.axis_index("tensor")}
    greet([other])
    copies = [remote(ins[i], outs[i], send.at[i], recv.at[i], other) for i in range(count)]
    for copy in copies:
        copy.start()
    for copy in copies:
        copy.wait()


def swap(ident, *arrays):
    count = len(arrays)
    return call(
        functools.partial(swap_kernel, count),
        ident,
        [shape_of(array) for array in arrays],
        [pltpu.SemaphoreType.DMA((count,)), pltpu.SemaphoreType.DMA((count,))],
        *arrays,
    )


def gather_kernel(n, shard, rows_a, rows_b, full, other_a, other_b, send, recv, pair_send, pair_recv, own):
    me = lax.axis_index("dp")
    other = {"tensor": 1 - lax.axis_index("tensor")}
    bits = bits_below(n)
    greet([{"dp": flip(me, bit)} for bit in bits] + [other])
    pair = [
        remote(rows_a, other_a, pair_send.at[0], pair_recv.at[0], other),
        remote(rows_b, other_b, pair_send.at[1], pair_recv.at[1], other),
    ]

    def hop(mask, bit):
        owner = flip(me, mask)
        src = shard if mask == 0 else full.at[owner]
        index = mask | bit
        return remote(
            src, full.at[owner], send.at[index], recv.at[index], {"dp": flip(me, bit)}
        )

    keep = pltpu.make_async_copy(shard, full.at[me], own)
    order = sorted(range(n), key=lambda mask: (-low_bit(mask, n), mask))
    sent = []
    for mask in order:
        if mask:
            bit = low_bit(mask, n)
            hop(mask ^ bit, bit).wait_recv()
        for bit in reversed(bits_below(low_bit(mask, n))):
            copy = hop(mask, bit)
            copy.start()
            sent.append(copy)
        if mask == 0:
            for copy in pair:
                copy.start()
            keep.start()
    keep.wait()
    for copy in sent:
        copy.wait_send()
    for copy in pair:
        copy.wait()


def gather(n, shard, rows_a, rows_b):
    return call(
        functools.partial(gather_kernel, n),
        1,
        [
            jax.ShapeDtypeStruct((n,) + shard.shape, shard.dtype),
            shape_of(rows_a),
            shape_of(rows_b),
        ],
        [
            pltpu.SemaphoreType.DMA((n,)),
            pltpu.SemaphoreType.DMA((n,)),
            pltpu.SemaphoreType.DMA((2,)),
            pltpu.SemaphoreType.DMA((2,)),
            pltpu.SemaphoreType.DMA,
        ],
        shard,
        rows_a,
        rows_b,
    )


def everyone(n, me):
    return [{"dp": lax.rem(me + k, n)} for k in range(1, n)] + [
        {"tensor": 1 - lax.axis_index("tensor")}
    ]


def dispatch_kernel(n, in_a, in_b, out_a, out_b, send, recv, pair_send, pair_recv, own):
    me = lax.axis_index("dp")
    half = lax.axis_index("tensor")
    other = {"tensor": 1 - half}
    width = in_a.shape[2]
    columns = pl.ds(pl.multiple_of(half * width, 128), width)
    ins, outs = (in_a, in_b), (out_a, out_b)
    greet(everyone(n, me))

    def direct(i, k):
        peer = lax.rem(me + k, n)
        return remote(
            ins[i].at[peer],
            outs[i].at[me, :, columns],
            send.at[i, k],
            recv.at[i, k],
            {"dp": peer},
        )

    def onward(i, k):
        part = outs[i].at[lax.rem(me - k + n, n), :, columns]
        return remote(part, part, pair_send.at[i, k], pair_recv.at[i, k], other)

    keep = [
        pltpu.make_async_copy(ins[i].at[me], outs[i].at[me, :, columns], own.at[i])
        for i in range(2)
    ]
    for i in range(2):
        keep[i].start()
        for k in range(1, n):
            direct(i, k).start()
    for i in range(2):
        keep[i].wait()
        onward(i, 0).start()
        for k in range(1, n):
            direct(i, k).wait_recv()
            onward(i, k).start()
    for i in range(2):
        for k in range(1, n):
            direct(i, k).wait_send()
        for k in range(n):
            onward(i, k).wait()


def dispatch(n, rows_a, rows_b):
    full = jax.ShapeDtypeStruct(rows_a.shape[:2] + (2 * rows_a.shape[2],), rows_a.dtype)
    return call(
        functools.partial(dispatch_kernel, n),
        2,
        [full, full],
        [pltpu.SemaphoreType.DMA((2, n)) for _ in range(4)] + [pltpu.SemaphoreType.DMA((2,))],
        rows_a,
        rows_b,
    )


def combine_kernel(
    n, in_a, in_b, out_a, out_b, got_a, got_b, sum_a, sum_b, send, recv, pair_send, pair_recv, own
):
    me = lax.axis_index("dp")
    half = lax.axis_index("tensor")
    other = {"tensor": 1 - half}
    width = out_a.shape[2]
    theirs = pl.ds(pl.multiple_of((1 - half) * width, 128), width)
    mine = pl.ds(pl.multiple_of(half * width, 128), width)
    ins, outs, gots, sums = (in_a, in_b), (out_a, out_b), (got_a, got_b), (sum_a, sum_b)
    greet(everyone(n, me))

    def across(i, k):
        block = lax.rem(me + k, n)
        return remote(
            ins[i].at[block, :, theirs],
            gots[i].at[block],
            pair_send.at[i, k],
            pair_recv.at[i, k],
            other,
        )

    def home(i, k):
        block = lax.rem(me + k, n)
        return remote(
            sums[i].at[block], outs[i].at[me], send.at[i, k], recv.at[i, k], {"dp": block}
        )

    order = list(range(1, n)) + [0]
    for i in range(2):
        for k in order:
            across(i, k).start()
    for i in range(2):
        for k in order:
            across(i, k).wait_recv()
            block = lax.rem(me + k, n)
            kept = ins[i][block, :, mine].astype(jnp.float32)
            total = (kept + gots[i][block].astype(jnp.float32)).astype(jnp.bfloat16)
            if k:
                sums[i][block] = total
                home(i, k).start()
            else:
                outs[i][block] = total
    for i in range(2):
        for k in range(n):
            across(i, k).wait_send()
        for k in range(1, n):
            home(i, k).wait()


def combine(n, parts_a, parts_b):
    size = parts_a.shape[:2] + (parts_a.shape[2] // 2,)
    out = jax.ShapeDtypeStruct(size, parts_a.dtype)
    return call(
        functools.partial(combine_kernel, n),
        3,
        [out, out],
        [pltpu.VMEM(size, parts_a.dtype) for _ in range(4)]
        + [pltpu.SemaphoreType.DMA((2, n)) for _ in range(4)]
        + [pltpu.SemaphoreType.DMA((2,))],
        parts_a,
        parts_b,
    )


def reduce_kernel(
    n, small, grads, rows, out, out_small, out_rows, got, stage, mine, theirs, send, recv, pair_send, pair_recv
):
    me = lax.axis_index("dp")
    other = {"tensor": 1 - lax.axis_index("tensor")}
    greet([{"dp": flip(me, bit)} for bit in bits_below(n)] + [other])
    pair_rows = remote(rows, out_rows, pair_send.at[0], pair_recv.at[0], other)
    pair_rows.start()

    def hop(mask):
        bit = low_bit(mask, n)
        src = grads.at[flip(me, mask)] if bit == 1 else stage.at[mask]
        return remote(src, got.at[mask], send.at[mask], recv.at[mask], {"dp": flip(me, bit)})

    def total(mask):
        value = grads[flip(me, mask)].astype(jnp.float32)
        for bit in bits_below(low_bit(mask, n)):
            hop(mask | bit).wait_recv()
            value = value + got[mask | bit].astype(jnp.float32)
        return value

    order = sorted(
        range(1, n), key=lambda mask: (low_bit(mask, n), low_bit(mask ^ low_bit(mask, n), n))
    )
    for mask in order:
        if low_bit(mask, n) > 1:
            stage[mask] = total(mask).astype(stage.dtype)
        hop(mask).start()
    value = total(0)
    out[...] = value
    mine[...] = value[:, value.shape[1] - small :]
    pair_small = remote(mine, theirs, pair_send.at[1], pair_recv.at[1], other)
    pair_small.start()
    for mask in order:
        hop(mask).wait_send()
    pair_small.wait()
    out_small[...] = mine[...] + theirs[...]
    pair_rows.wait()


def reduce(n, small, grads, rows):
    depth, columns = grads.shape[1:]
    return call(
        functools.partial(reduce_kernel, n, small),
        4,
        [
            jax.ShapeDtypeStruct((depth, columns), jnp.float32),
            jax.ShapeDtypeStruct((depth, small), jnp.float32),
            shape_of(rows),
        ],
        [
            pltpu.VMEM(grads.shape, grads.dtype),
            pltpu.VMEM(grads.shape, grads.dtype),
            pltpu.VMEM((depth, small), jnp.float32),
            pltpu.VMEM((depth, small), jnp.float32),
            pltpu.SemaphoreType.DMA((n,)),
            pltpu.SemaphoreType.DMA((n,)),
            pltpu.SemaphoreType.DMA((2,)),
            pltpu.SemaphoreType.DMA((2,)),
        ],
        grads,
        rows,
    )


def in_order(half, mine, theirs, axis):
    first = jnp.where(half == 0, mine, theirs)
    second = jnp.where(half == 0, theirs, mine)
    return jnp.concatenate([first, second], axis=axis)


def norm_rows(values, gain, shift):
    centre = values - jnp.mean(values, axis=-1, keepdims=True)
    spread = jnp.mean(centre * centre, axis=-1, keepdims=True)
    return centre * lax.rsqrt(spread + 1e-06) * gain + shift


def softmax_rows(query, key_rows):
    scores = lax.dot_general(
        query, key_rows, (((1,), (1,)), ((), ())), preferred_element_type=jnp.float32
    ) * DH ** (-0.5)
    powers = jnp.exp(scores - jnp.max(scores, axis=-1, keepdims=True))
    return powers / jnp.sum(powers, axis=-1, keepdims=True)


def attend_kernel(wide, normed, full, mixed, heads_out, branch):
    for image in range(normed.shape[0]):
        mixed[image] = jnp.dot(
            normed[image], full[:, : 3 * wide], preferred_element_type=jnp.float32
        ).astype(jnp.bfloat16)
        outs = []
        for at in range(0, wide, DH):
            query, key_rows, value_rows = (
                mixed[image, :, part * wide + at : part * wide + at + DH] for part in range(3)
            )
            weights = softmax_rows(query, key_rows).astype(jnp.bfloat16)
            outs.append(jnp.dot(weights, value_rows, preferred_element_type=jnp.float32))
        heads_out[image] = jnp.concatenate(outs, axis=1).astype(jnp.bfloat16)
        branch[image] = lax.dot_general(
            heads_out[image],
            full[:, 3 * wide : 4 * wide],
            (((1,), (1,)), ((), ())),
            preferred_element_type=jnp.float32,
        ).astype(jnp.bfloat16)


def attend_back_kernel(
    wide, normed, mixed, heads_out, grad_branch, full, grads, grad_part, grad_mixed, grad_heads
):
    rows = (((0,), (0,)), ((), ()))
    cols = (((1,), (1,)), ((), ()))
    f32 = jnp.float32
    scale = DH ** (-0.5)
    for image in range(normed.shape[0]):
        grad_heads[image] = jnp.dot(
            grad_branch[image], full[:, 3 * wide : 4 * wide], preferred_element_type=f32
        ).astype(jnp.bfloat16)
        parts = ([], [], [])
        for at in range(0, wide, DH):
            query, key_rows, value_rows = (
                mixed[image, :, part * wide + at : part * wide + at + DH] for part in range(3)
            )
            probs = softmax_rows(query, key_rows)
            grad_out = grad_heads[image, :, at : at + DH]
            grad_probs = lax.dot_general(grad_out, value_rows, cols, preferred_element_type=f32)
            parts[2].append(
                lax.dot_general(
                    probs.astype(jnp.bfloat16), grad_out, rows, preferred_element_type=f32
                )
            )
            grad_scores = (
                probs * (grad_probs - jnp.sum(probs * grad_probs, axis=-1, keepdims=True))
            ).astype(jnp.bfloat16)
            parts[0].append(jnp.dot(grad_scores, key_rows, preferred_element_type=f32) * scale)
            parts[1].append(
                lax.dot_general(grad_scores, query, rows, preferred_element_type=f32) * scale
            )
        grad_mixed[image] = jnp.concatenate(parts[0] + parts[1] + parts[2], axis=1).astype(
            jnp.bfloat16
        )
        grad_part[image] = lax.dot_general(
            grad_mixed[image], full[:, : 3 * wide], cols, preferred_element_type=f32
        )
    images = range(normed.shape[0])
    grads[:, : 3 * wide] = sum(
        lax.dot_general(normed[i], grad_mixed[i], rows, preferred_element_type=f32) for i in images
    ).astype(jnp.bfloat16)
    grads[:, 3 * wide : 4 * wide] = sum(
        lax.dot_general(grad_branch[i], heads_out[i], rows, preferred_element_type=f32)
        for i in images
    ).astype(jnp.bfloat16)


def local_call(kernel, outs, scratch, *operands):
    return pl.pallas_call(
        kernel,
        out_shape=outs,
        in_specs=[VMEM] * len(operands),
        out_specs=[VMEM] * len(outs),
        scratch_shapes=scratch,
        compiler_params=pltpu.CompilerParams(vmem_limit_bytes=LIMIT),
    )(*operands)


def attend(normed, full, wide):
    images, length, width = normed.shape
    sizes = ((images, length, 3 * wide), (images, length, wide), (images, length, width))
    return local_call(
        functools.partial(attend_kernel, wide),
        [jax.ShapeDtypeStruct(size, jnp.bfloat16) for size in sizes],
        [],
        normed,
        full,
    )


def attend_back(normed, mixed, heads_out, grad_branch, full, wide):
    images, length, width = normed.shape
    return local_call(
        functools.partial(attend_back_kernel, wide),
        [
            jax.ShapeDtypeStruct((width, 4 * wide), jnp.bfloat16),
            jax.ShapeDtypeStruct(normed.shape, jnp.float32),
        ],
        [pltpu.VMEM(mixed.shape, mixed.dtype), pltpu.VMEM(heads_out.shape, heads_out.dtype)],
        normed,
        mixed,
        heads_out,
        grad_branch,
        full,
    )


def body(
    tokens,
    w_qkv,
    w_mix,
    w_router,
    gain_one,
    shift_one,
    gain_two,
    shift_two,
    w_expand,
    w_shrink,
    expert_ids,
    slot_ids,
    keep_mask,
    out_grad,
):
    highest = lax.Precision.HIGHEST
    contract_rows = (((0,), (0,)), ((), ()))
    contract_cols = (((1,), (1,)), ((), ()))
    bf16 = jnp.bfloat16
    f32 = jnp.float32
    rows, width = tokens.shape
    group = expert_ids.shape[0]
    experts = lax.axis_size("dp")
    half = lax.axis_index("tensor")
    slots = 2 * max(1, 2 * group * 2 // 3 // experts)
    depth = w_qkv.shape[0]
    qkv_cols = 3 * w_qkv.shape[2]
    mix_cols = w_mix.shape[1]
    half_width = width // 2
    small = -(-(experts + 4) // 128) * 128

    vectors = jnp.stack([gain_one, shift_one, gain_two, shift_two], axis=1)
    shard = jnp.concatenate(
        [
            w_qkv.reshape(depth, qkv_cols),
            w_mix,
            w_router,
            vectors,
            jnp.zeros((depth, small - experts - 4), bf16),
        ],
        axis=1,
    )
    full, tokens_other, grad_other = gather(experts, shard, tokens, out_grad)
    full = full.reshape(experts * depth, -1)
    router_full = full[:, qkv_cols + mix_cols : qkv_cols + mix_cols + experts]
    vectors = full[:, qkv_cols + mix_cols + experts : qkv_cols + mix_cols + experts + 4]
    gain_a, shift_a, gain_b, shift_b = vectors.astype(f32).T
    resid = in_order(half, tokens, tokens_other, 0).astype(f32)
    grad_group = in_order(half, out_grad, grad_other, 0).astype(f32)

    pictures = jnp.where(
        half == 0, jnp.stack([tokens, tokens_other]), jnp.stack([tokens_other, tokens])
    ).astype(f32)
    normed_a = norm_rows(pictures, gain_a, shift_a).astype(bf16)
    mixed, heads_out, branch = attend(normed_a, full, mix_cols)
    (branch_other,) = swap(5, branch)
    resid_b = resid + (branch.astype(f32) + branch_other.astype(f32)).reshape(group, width)
    group_b = norm_rows(resid_b, gain_b, shift_b).astype(bf16)

    logits = jnp.dot(group_b, router_full, preferred_element_type=f32)
    onehot = expert_ids[:, :, None] == jnp.arange(experts, dtype=jnp.int32)[None, None, :]
    chosen = jnp.sum(jnp.where(onehot, logits[:, None, :], 0.0), axis=-1)
    pick = jax.nn.softmax(chosen, axis=-1)
    keep_float = keep_mask.astype(f32)
    gates = pick * keep_float
    dest = jnp.where(keep_mask > 0, expert_ids * slots + slot_ids, experts * slots)
    places = jnp.arange(experts * slots, dtype=jnp.int32)[None, :]
    spread = [(dest[:, j : j + 1] == places).astype(bf16) for j in range(2)]
    spread_both = spread[0] + spread[1]

    def my_columns(values):
        return lax.dynamic_slice_in_dim(values, half * half_width, half_width, 1)

    rows_sent = lax.dot_general(
        spread_both, my_columns(group_b), contract_rows, preferred_element_type=f32
    ).astype(bf16)
    grad_cols = my_columns(grad_group)
    grads_sent = sum(
        lax.dot_general(
            spread[j],
            (gates[:, j : j + 1] * grad_cols).astype(bf16),
            contract_rows,
            preferred_element_type=f32,
        )
        for j in range(2)
    ).astype(bf16)
    arrived, grad_result = dispatch(
        experts,
        rows_sent.reshape(experts, slots, half_width),
        grads_sent.reshape(experts, slots, half_width),
    )
    arrived = arrived.reshape(-1, width)
    grad_result = grad_result.reshape(-1, width)

    expand_here = w_expand[0]
    shrink_here = w_shrink[0]
    inner = jnp.dot(arrived, expand_here, preferred_element_type=f32)
    gelu_value, gelu_pull = jax.vjp(jax.nn.gelu, inner)
    active = gelu_value.astype(bf16)
    result = jnp.dot(active, shrink_here, preferred_element_type=f32).astype(bf16)
    grad_active = lax.dot_general(
        grad_result, shrink_here, contract_cols, preferred_element_type=f32
    )
    grad_inner = gelu_pull(grad_active)[0].astype(bf16)
    grad_arrived = lax.dot_general(
        grad_inner, expand_here, contract_cols, preferred_element_type=f32
    ).astype(bf16)
    back, grad_back = combine(
        experts,
        result.reshape(experts, slots, width),
        grad_arrived.reshape(experts, slots, width),
    )
    grad_shrink = lax.dot_general(active, grad_result, contract_rows, preferred_element_type=f32)
    grad_expand = lax.dot_general(arrived, grad_inner, contract_rows, preferred_element_type=f32)

    back = back.reshape(-1, half_width)
    grad_back = grad_back.reshape(-1, half_width)
    route_out = [jnp.dot(spread[j], back, preferred_element_type=f32) for j in range(2)]
    branch_cols = (gates[:, 0:1] * route_out[0] + gates[:, 1:2] * route_out[1]).astype(bf16)
    gate_part = jnp.stack([jnp.sum(grad_cols * route_out[j], axis=-1) for j in range(2)], axis=0)
    grad_cols_b = jnp.dot(spread_both, grad_back, preferred_element_type=f32).astype(bf16)
    trade = [(0, 1), (1, 0)]
    branch_theirs = lax.ppermute(branch_cols, "tensor", trade)
    grad_theirs = lax.ppermute(grad_cols_b, "tensor", trade)
    gate_theirs = lax.ppermute(gate_part, "tensor", trade)
    grad_gate = (gate_part + gate_theirs).T
    branch_b = in_order(half, branch_cols, branch_theirs, 1).astype(f32)
    grad_routes = in_order(half, grad_cols_b, grad_theirs, 1).astype(f32)
    block_out = lax.dynamic_slice_in_dim(resid_b + branch_b, half * rows, rows, 0).astype(bf16)

    grad_pick = keep_float * grad_gate
    grad_chosen = pick * (grad_pick - jnp.sum(pick * grad_pick, axis=-1, keepdims=True))
    grad_logits = jnp.sum(jnp.where(onehot, grad_chosen[:, :, None], 0.0), axis=1)
    grad_router = lax.dot_general(
        group_b.astype(f32), grad_logits, contract_rows, precision=highest
    )
    grad_normed_b = grad_routes + lax.dot_general(
        grad_logits, router_full.astype(f32), contract_cols, precision=highest
    )
    norm_value_b, norm_pull_b = jax.vjp(norm_rows, resid_b, gain_b, shift_b)
    grad_resid_b, grad_gain_b, grad_shift_b = norm_pull_b(grad_normed_b)
    grad_resid_b = grad_resid_b + grad_group

    grad_branch = grad_resid_b.astype(bf16).reshape(pictures.shape)
    grad_weights, grad_part = attend_back(
        normed_a, mixed, heads_out, grad_branch, full, mix_cols
    )
    norm_value_a, norm_pull_a = jax.vjp(norm_rows, pictures, gain_a, shift_a)
    grad_gain_a, grad_shift_a = norm_pull_a(grad_part)[1:]
    grads = jnp.concatenate(
        [
            grad_weights,
            (0.5 * grad_router).astype(bf16),
            jnp.stack(
                [grad_gain_a, grad_shift_a, 0.5 * grad_gain_b, 0.5 * grad_shift_b], axis=1
            ).astype(bf16),
            jnp.zeros((width, small - experts - 4), bf16),
        ],
        axis=1,
    ).reshape(experts, depth, -1)
    part_theirs = jnp.where(half == 0, grad_part[1], grad_part[0]).astype(bf16)
    summed, summed_small, part_got = reduce(experts, small, grads, part_theirs)
    summed_small = lax.dynamic_slice_in_dim(summed_small, half * (depth // 2), depth // 2, 0)
    grad_normed_a = jnp.where(half == 0, grad_part[0], grad_part[1]) + part_got.astype(f32)
    own = tokens.astype(f32)
    own_value, own_pull = jax.vjp(lambda values: norm_rows(values, gain_a, shift_a), own)
    grad_tokens = own_pull(grad_normed_a)[0] + lax.dynamic_slice_in_dim(
        grad_resid_b, half * rows, rows, 0
    )
    return (
        block_out,
        grad_tokens,
        summed[:, :qkv_cols].reshape(depth, 3, -1),
        summed[:, qkv_cols : qkv_cols + mix_cols],
        summed_small[:, :experts],
        summed_small[:, experts],
        summed_small[:, experts + 1],
        summed_small[:, experts + 2],
        summed_small[:, experts + 3],
        grad_expand[None],
        grad_shrink[None],
    )


def solution(mesh):
    placed = (
        P(("dp", "tensor"), None),
        P("dp", None, "tensor"),
        P("dp", "tensor"),
        P("dp", None),
        P("dp"),
        P("dp"),
        P("dp"),
        P("dp"),
        P("dp", None, "tensor"),
        P("dp", "tensor", None),
        P("dp", None),
        P("dp", None),
        P("dp", None),
        P(("dp", "tensor"), None),
    )
    return jax.shard_map(
        body,
        mesh=mesh,
        in_specs=placed,
        out_specs=(
            P(("dp", "tensor"), None),
            P(("dp", "tensor"), None),
            P("dp", None, "tensor"),
            P("dp", "tensor"),
            P(("dp", "tensor"), None),
            P(("dp", "tensor")),
            P(("dp", "tensor")),
            P(("dp", "tensor")),
            P(("dp", "tensor")),
            P("dp", None, "tensor"),
            P("dp", "tensor", None),
        ),
        check_vma=False,
    )
```

profile of v0, /device:TPU:0, one launch (start us, length us, event | category | flops | bytes accessed | tf_op | source)
XLA Modules:
  0.0 293.1 jit_solution(9351929050965639595)
XLA Ops:
  8.4 25.9 %shard_map.221 = (bf16[16,48,1664]{2,1,0:T(8,128)(2,1)S(1)}, bf16[197,768]{1,0:T(8,128)(2,1)S(1)}, bf16[197,768]{1,0:T(8,128)(2,1)S(1)}) custom-call(bf16[48,1664]{1,0:T(8,128)(2,1)S(1)} %concatenate.19.shard, bf16[197,768]{1,0:T(8,128)(2,1)S(1)} %copy-done.2, bf16[197,768]{1,0:T(8,128)(2,1)S(1)} %copy-done.15), custom_call_target="tpu_custom_call" | custom-call | tf_op jit(solution)/shard_map/pallas_call | solution.py:58
  40.0 4.1 %shard_map.222 = (bf16[2,197,1152]{2,1,0:T(8,128)(2,1)S(1)}, bf16[2,197,384]{2,1,0:T(8,128)(2,1)S(1)}, bf16[2,197,768]{2,1,0:T(8,128)(2,1)S(1)}) custom-call(bf16[2,197,768]{2,1,0:T(8,128)(2,1)S(1)} %fusion.34.normed, bf16[768,1664]{1,0:T(8,128)(2,1)S(1)} %bitcast.88), custom_call_target="tpu_custom_call" | custom-call | tf_op jit(solution)/shard_map/pallas_call | solution.py:440
  44.1 16.6 %shard_map.223 = bf16[2,197,768]{2,1,0:T(8,128)(2,1)S(1)} custom-call(bf16[2,197,768]{2,1,0:T(8,128)(2,1)S(1)} %get-tuple-element.28.refs_0_), custom_call_target="tpu_custom_call" | custom-call | tf_op jit(solution)/shard_map/pallas_call | solution.py:58
  63.7 2.4 reshape.208
  66.2 2.1 fusion.75
  70.1 2.4 reshape.196
  72.6 2.9 add_convert_fusion.1
  77.7 2.2 maximum_convert_fusion.1
  79.9 2.0 convolution_convert_fusion
  83.8 46.8 %shard_map.224 = (bf16[16,64,768]{2,1,0:T(8,128)(2,1)S(1)}, bf16[16,64,768]{2,1,0:T(8,128)(2,1)S(1)}) custom-call(bf16[16,64,384]{2,1,0:T(8,128)(2,1)S(1)} %bitcast.98, bf16[16,64,384]{2,1,0:T(8,128)(2,1)S(1)} %bitcast.99), custom_call_target="tpu_custom_call" | custom-call | tf_op jit(solution)/shard_map/pallas_call | solution.py:58
  130.7 2.6 fusion.15
  133.3 3.9 %fusion.20 = bf16[1024,768]{1,0:T(8,128)(2,1)S(1)} fusion(bf16[1,1536,768]{2,1,0:T(8,128)(2,1)S(1)} %copy-done, f32[1024,1536]{1,0:T(8,128)S(1)} %fusion.15), kind=kOutput, calls=%fused_computation.22 | convolution fusion | flops 2430861312 | bytes 10223616 | tf_op jit(solution)/shard_map/dot_general | solution.py:579
  137.3 6.4 %fusion.6 = bf16[1024,1536]{1,0:T(8,128)(2,1)S(1)} fusion(f32[1024,1536]{1,0:T(8,128)S(1)} %fusion.15, bf16[1024,768]{1,0:T(8,128)(2,1)S(1)} %bitcast.100, bf16[1,1536,768]{2,1,0:T(8,128)(2,1)S(1)} %copy-done), kind=kOutput, calls=%fused_computation.8 | convolution fusion | flops 2447376384 | bytes 13369344 | tf_op jit(solution)/shard_map/dot_general | solution.py:580
  143.6 2.6 fusion.17
  146.3 48.7 %shard_map.225 = (bf16[16,64,384]{2,1,0:T(8,128)(2,1)S(1)}, bf16[16,64,384]{2,1,0:T(8,128)(2,1)S(1)}) custom-call(bf16[16,64,768]{2,1,0:T(8,128)(2,1)S(1)} %bitcast.96, bf16[16,64,768]{2,1,0:T(8,128)(2,1)S(1)} %bitcast.97), custom_call_target="tpu_custom_call" | custom-call | tf_op jit(solution)/shard_map/pallas_call | solution.py:58
  201.5 4.4 %convolution_bitcast_fusion.1 = f32[1,768,1536]{2,1,0:T(8,128)} fusion(bf16[1024,768]{1,0:T(8,128)(2,1)S(1)} %bitcast.95, bf16[1024,1536]{1,0:T(8,128)(2,1)S(1)} %fusion.6), kind=kOutput, calls=%fused_computation.11 | convolution fusion | flops 2415919104 | bytes 9437184 | tf_op jit(solution)/shard_map/dot_general | solution.py:593
  205.8 16.1 %convolution_bitcast_fusion = f32[1,1536,768]{2,1,0:T(8,128)} fusion(bf16[1024,768]{1,0:T(8,128)(2,1)S(1)} %bitcast.101, f32[1024,1536]{1,0:T(8,128)S(1)} %bitcast.132), kind=kOutput, calls=%fused_computation.10 | convolution fusion | flops 2430074880 | bytes 12582912 | tf_op jit(solution)/shard_map/dot_general | solution.py:592
  224.1 2.1 multiply_reduce_fusion
  231.8 10.9 %shard_map.226 = (bf16[768,1536]{1,0:T(8,128)(2,1)S(1)}, f32[2,197,768]{2,1,0:T(8,128)S(1)}) custom-call(bf16[2,197,768]{2,1,0:T(8,128)(2,1)S(1)} %copy-done.8, bf16[2,197,1152]{2,1,0:T(8,128)(2,1)S(1)} %copy-done.18, bf16[2,197,384]{2,1,0:T(8,128)(2,1)S(1)} %get-tuple-element.34.heads_out, bf16[2,197,768]{2,1,0:T(8,128)(2,1)S(1)} %copy-done.13, ...), custom_call_target="tpu_custom_call" | custom-call | tf_op jit(solution)/shard_map/pallas_call | solution.py:440
  244.4 5.2 %concatenate.24 = bf16[768,1664]{1,0:T(8,128)(2,1)} concatenate(bf16[768,1536]{1,0:T(8,128)(2,1)} %copy-done.14, bf16[768,16]{1,0:T(8,128)(2,1)S(1)} %fusion.37, bf16[768,1]{1,0:T(8,128)(2,1)S(1)} %stack.60, bf16[768,1]{1,0:T(8,128)(2,1)S(1)} %stack.61, bf16[768,1]{1,0:T(8,128)(2,1)S(1)} %mul.348, bf16[768,1]{1,0:T(8,128)(2,1)S(1)} %mul.349, bf16[768,108]{1,0:T(8,128)(2,1)S(1)} %broadcast_in_dim.75), dimensions={1} | concatenate | bytes 5111808 | tf_op jit(solution)/shard_map/concatenate | solution.py:629
  249.6 1.7 copy-done.6
  251.3 32.0 %shard_map.227 = (f32[48,1664]{1,0:T(8,128)S(1)}, f32[48,128]{1,0:T(8,128)S(1)}, bf16[197,768]{1,0:T(8,128)(2,1)S(1)}) custom-call(bf16[16,48,1664]{2,1,0:T(8,128)(2,1)S(1)} %bitcast.89, bf16[197,768]{1,0:T(8,128)(2,1)S(1)} %fusion.56.rows), custom_call_target="tpu_custom_call" | custom-call | tf_op jit(solution)/shard_map/pallas_call | solution.py:58
  288.0 2.1 fusion.54
  290.1 2.0 dynamic-slice_add_fusion.1
  (151 shorter events, 43.5 us)
Async XLA Ops:
  0.6 132.6 %copy-start = (bf16[1,1536,768]{2,1,0:T(8,128)(2,1)S(1)}, bf16[1,1536,768]{2,1,0:T(8,128)(2,1)}, u32[]{:S(2)}) copy-start(bf16[1,1536,768]{2,1,0:T(8,128)(2,1)} %param.23) | copy-start | bytes 7077892
  8.4 28.9 %copy-start.3 = (bf16[197,768]{1,0:T(8,128)(2,1)S(1)}, bf16[197,768]{1,0:T(8,128)(2,1)}, u32[]{:S(2)}) copy-start(bf16[197,768]{1,0:T(8,128)(2,1)} %rows_a.1) | copy-start | bytes 907780
  40.0 4.1 %copy-start.7 = (bf16[2,197,768]{2,1,0:T(8,128)(2,1)}, bf16[2,197,768]{2,1,0:T(8,128)(2,1)S(1)}, u32[]{:S(2)}) copy-start(bf16[2,197,768]{2,1,0:T(8,128)(2,1)S(1)} %fusion.34.normed) | copy-start | bytes 1815556
  40.0 20.7 %copy-start.16 = (bf16[197,768]{1,0:T(8,128)(2,1)S(1)}, bf16[197,768]{1,0:T(8,128)(2,1)}, u32[]{:S(2)}) copy-start(bf16[197,768]{1,0:T(8,128)(2,1)} %rows_b.1) | copy-start | bytes 907780
  40.0 20.8 %copy-start.20 = (bf16[197,768]{1,0:T(8,128)(2,1)S(1)}, bf16[197,768]{1,0:T(8,128)(2,1)}, u32[]{:S(2)}) copy-start(bf16[197,768]{1,0:T(8,128)(2,1)} %copy-done.19) | copy-start | bytes 907780
  44.1 17.6 %copy-start.9 = (bf16[2,197,768]{2,1,0:T(8,128)(2,1)}, bf16[2,197,768]{2,1,0:T(8,128)(2,1)S(1)}, u32[]{:S(2)}) copy-start(bf16[2,197,768]{2,1,0:T(8,128)(2,1)S(1)} %get-tuple-element.28.refs_0_) | copy-start | bytes 1815556
  44.1 17.6 %copy-start.17 = (bf16[2,197,1152]{2,1,0:T(8,128)(2,1)}, bf16[2,197,1152]{2,1,0:T(8,128)(2,1)S(1)}, u32[]{:S(2)}) copy-start(bf16[2,197,1152]{2,1,0:T(8,128)(2,1)S(1)} %get-tuple-element.33.mixed) | copy-start | bytes 2723332
  66.1 2.1 copy-start.12
  66.2 2.4 copy-start.21
  69.9 2.6 copy-start.31
  69.9 2.6 copy-start.32
  69.9 2.6 copy-start.33
  82.8 47.8 %copy-start.34 = (bf16[1,768,1536]{2,1,0:T(8,128)(2,1)S(1)}, bf16[1,768,1536]{2,1,0:T(8,128)(2,1)}, u32[]{:S(2)}) copy-start(bf16[1,768,1536]{2,1,0:T(8,128)(2,1)} %param.22) | copy-start | bytes 7077892
  133.3 4.0 %copy-start.35 = (f32[1024,1536]{1,0:T(8,128)}, f32[1024,1536]{1,0:T(8,128)S(1)}, u32[]{:S(2)}) copy-start(f32[1024,1536]{1,0:T(8,128)S(1)} %fusion.15) | copy-start | bytes 18874372
  197.0 89.8 %collective-permute-start = (bf16[394,384]{1,0:T(8,128)(2,1)}, bf16[394,384]{1,0:T(8,128)(2,1)}, u32[]{:S(2)}, u32[]{:S(2)}) collective-permute-start(bf16[394,384]{1,0:T(8,128)(2,1)} %get-tuple-element.112), channel_id=1, source_target_pairs={{0,1},{1,0},{2,3},{3,2},{4,5},{5,4},{6,7},{7,6},{8,9},{9,8},{10,11... | collective-permute-start | bytes 907784 | tf_op jit(solution)/shard_map/ppermute | solution.py:602
  198.5 23.5 %collective-permute-start.2 = (f32[2,394]{1,0:T(2,128)S(1)}, f32[2,394]{1,0:T(2,128)S(1)}, u32[]{:S(2)}, u32[]{:S(2)}) collective-permute-start(f32[2,394]{1,0:T(2,128)S(1)} %pad_maximum_fusion), channel_id=1, source_target_pairs={{0,1},{1,0},{2,3},{3,2},{4,5},{5,4},{6,7},{7,6},{8,9},{9,8},{10,11... | collective-permute-start | bytes 9464 | tf_op jit(solution)/shard_map/ppermute | solution.py:604
  199.1 6.7 %slice-start = ((s8[6291456]{0:T(1024)(128)(4,1)}), s8[4194304]{0:T(1024)(128)(4,1)S(1)}, s32[]{:S(2)}) async-start(s8[6291456]{0:T(1024)(128)(4,1)} %bitcast.131), calls=%async_computation | async-start | bytes 8388608
  199.8 23.2 %collective-permute-start.1 = (bf16[394,384]{1,0:T(8,128)(2,1)S(1)}, bf16[394,384]{1,0:T(8,128)(2,1)}, u32[]{:S(2)}, u32[]{:S(2)}) collective-permute-start(bf16[394,384]{1,0:T(8,128)(2,1)S(1)} %convolution_convert_fusion.1), channel_id=1, source_target_pairs={{0,1},{1,0},{2,3},{3,2},{4,5},{5,4},{6,7},{7,6},{8,9},{9,8},{10,11... | collective-permute-start | bytes 907784 | tf_op jit(solution)/shard_map/ppermute | solution.py:603
  201.5 4.4 %slice-start.1 = ((s8[6291456]{0:T(1024)(128)(4,1)}), s8[2097152]{0:T(1024)(128)(4,1)S(1)}, s32[]{:S(2)}) async-start(s8[6291456]{0:T(1024)(128)(4,1)} %bitcast.131), calls=%async_computation.1 | async-start | bytes 4194304
  205.8 16.2 %copy-start.24 = (bf16[394,768]{1,0:T(8,128)(2,1)S(1)}, bf16[394,768]{1,0:T(8,128)(2,1)}, u32[]{:S(2)}) copy-start(bf16[394,768]{1,0:T(8,128)(2,1)} %copy-done.23) | copy-start | bytes 1815556
  222.0 2.1 copy-start.22
  227.3 2.3 copy-start.18
  286.2 4.0 %copy-start.29 = (f32[197,768]{1,0:T(8,128)S(1)}, f32[197,768]{1,0:T(8,128)}, u32[]{:S(2)}) copy-start(f32[197,768]{1,0:T(8,128)} %get-tuple-element.103) | copy-start | bytes 1815556
  288.0 4.9 %copy-start.1 = (bf16[1,1536,768]{2,1,0:T(8,128)(2,1)S(1)}, bf16[1,1536,768]{2,1,0:T(8,128)(2,1)}, u32[]{:S(2)}) copy-start(bf16[1,1536,768]{2,1,0:T(8,128)(2,1)} %param.23) | copy-start | bytes 7077892
  (17 other events, 20.7 us)
where the time goes:
time: 297 us; the launch traced here: 293 us
  Pallas kernels  185 us (62%)
  matrix products  47 us (16%)
  local copies, waits for them, and re-layouts  34 us (11%)
  other arithmetic  22.1 us (7%)
  starting transfers between devices  3.63 us (1%)
    pallas_call x5, Pallas kernels, call(): pl.pallas_call(kernel, out_shape=outs, in_specs=[VMEM] * len(operands), o...  170 us
    dot_general x1, matrix products, body(): lax.dot_general(active, grad_result, contract_rows, preferred_element_typ...  16.1 us
    pallas_call x2, Pallas kernels, local_call(): pl.pallas_call(kernel, out_shape=outs, in_specs=[VMEM] * len(operands), o...  15 us
    unnamed x78, local copies, waits for them, and re-layouts  14.3 us
    dot_general x1, matrix products, body(): lax.dot_general(grad_result, shrink_here, contract_cols, preferred_elemen...  6.37 us
  transfers between devices with their start and end apart: 3, of which 0 were waited for; matrix products, arithmetic and copies ran while one was open for 13% of the time, Pallas kernels for 15%

commit v1 on v0

--- a/solution.py
+++ b/solution.py
@@ -381,7 +381,8 @@
             weights = softmax_rows(query, key_rows).astype(jnp.bfloat16)
             outs.append(jnp.dot(weights, value_rows, preferred_element_type=jnp.float32))
         heads_out[image] = jnp.concatenate(outs, axis=1).astype(jnp.bfloat16)
-        branch[image] = lax.dot_general(
+        length = normed.shape[1]
+        branch[image * length : (image + 1) * length, :] = lax.dot_general(
             heads_out[image],
             full[:, 3 * wide : 4 * wide],
             (((1,), (1,)), ((), ())),
@@ -430,6 +431,7 @@
     grads[:, : 3 * wide] = sum(
         lax.dot_general(normed[i], grad_mixed[i], rows, preferred_element_type=f32) for i in images
     ).astype(jnp.bfloat16)
+    grads[:, 4 * wide :] = jnp.zeros((grads.shape[0], grads.shape[1] - 4 * wide), grads.dtype)
     grads[:, 3 * wide : 4 * wide] = sum(
         lax.dot_general(grad_branch[i], heads_out[i], rows, preferred_element_type=f32)
         for i in images
@@ -449,7 +451,7 @@
 
 def attend(normed, full, wide):
     images, length, width = normed.shape
-    sizes = ((images, length, 3 * wide), (images, length, wide), (images, length, width))
+    sizes = ((images, length, 3 * wide), (images, length, wide), (images * length, width))
     return local_call(
         functools.partial(attend_kernel, wide),
         [jax.ShapeDtypeStruct(size, jnp.bfloat16) for size in sizes],
@@ -464,7 +466,7 @@
     return local_call(
         functools.partial(attend_back_kernel, wide),
         [
-            jax.ShapeDtypeStruct((width, 4 * wide), jnp.bfloat16),
+            jax.ShapeDtypeStruct((width, full.shape[1]), jnp.bfloat16),
             jax.ShapeDtypeStruct(normed.shape, jnp.float32),
         ],
         [pltpu.VMEM(mixed.shape, mixed.dtype), pltpu.VMEM(heads_out.shape, heads_out.dtype)],
@@ -533,7 +535,7 @@
     normed_a = norm_rows(pictures, gain_a, shift_a).astype(bf16)
     mixed, heads_out, branch = attend(normed_a, full, mix_cols)
     (branch_other,) = swap(5, branch)
-    resid_b = resid + (branch.astype(f32) + branch_other.astype(f32)).reshape(group, width)
+    resid_b = resid + (branch.astype(f32) + branch_other.astype(f32))
     group_b = norm_rows(resid_b, gain_b, shift_b).astype(bf16)
 
     logits = jnp.dot(group_b, router_full, preferred_element_type=f32)
@@ -626,9 +628,8 @@
     )
     norm_value_a, norm_pull_a = jax.vjp(norm_rows, pictures, gain_a, shift_a)
     grad_gain_a, grad_shift_a = norm_pull_a(grad_part)[1:]
-    grads = jnp.concatenate(
+    small_grads = jnp.concatenate(
         [
-            grad_weights,
             (0.5 * grad_router).astype(bf16),
             jnp.stack(
                 [grad_gain_a, grad_shift_a, 0.5 * grad_gain_b, 0.5 * grad_shift_b], axis=1
@@ -636,7 +637,9 @@
             jnp.zeros((width, small - experts - 4), bf16),
         ],
         axis=1,
-    ).reshape(experts, depth, -1)
+    )
+    grads = lax.dynamic_update_slice(grad_weights, small_grads, (0, qkv_cols + mix_cols))
+    grads = grads.reshape(experts, depth, -1)
     part_theirs = jnp.where(half == 0, grad_part[1], grad_part[0]).astype(bf16)
     summed, summed_small, part_got = reduce(experts, small, grads, part_theirs)
     summed_small = lax.dynamic_slice_in_dim(summed_small, half * (depth // 2), depth // 2, 0)

time: 297 us -> 285 us (0.960)
  other arithmetic: 22.1 us -> 14.6 us
  local copies, waits for them, and re-layouts: 34 us -> 26.5 us
    unnamed x78 -> x62, local copies, waits for them, and re-layouts: 14.3 us -> 10 us
    concatenate x1, local copies, waits for them, and re-layouts: 5.17 us -> 2.16 us  [body(): jnp.concatenate([(0.5 * grad_router).astype(bf16), jnp.stack([grad_gain_a...]
  transfers between devices with their start and end apart: 3 -> 3, of which waited for: 0 -> 0; matrix products, arithmetic and copies ran while one was open for 13% -> 15% of each run, Pallas kernels for 15% -> 16%
where the time goes in v1:
time: 285 us; the launch traced here: 280 us
  Pallas kernels  187 us (66%)
  matrix products  47.6 us (17%)
  local copies, waits for them, and re-layouts  26.5 us (9%)
  other arithmetic  14.6 us (5%)
  starting transfers between devices  3.56 us (1%)
    pallas_call x5, Pallas kernels, call(): pl.pallas_call(kernel, out_shape=outs, in_specs=[VMEM] * len(operands), o...  170 us
    pallas_call x2, Pallas kernels, local_call(): pl.pallas_call(kernel, out_shape=outs, in_specs=[VMEM] * len(operands), o...  16.5 us
    dot_general x1, matrix products, body(): lax.dot_general(active, grad_result, contract_rows, preferred_element_typ...  14.9 us
    unnamed x62, local copies, waits for them, and re-layouts  10 us
    dot_general x1, matrix products, body(): lax.dot_general(grad_result, shrink_here, contract_cols, preferred_elemen...  6.34 us
  transfers between devices with their start and end apart: 3, of which 0 were waited for; matrix products, arithmetic and copies ran while one was open for 15% of the time, Pallas kernels for 16%

profile of v1, /device:TPU:0, one launch (start us, length us, event | category | flops | bytes accessed | tf_op | source)
XLA Modules:
  0.0 280.2 jit_solution(6027585083065257876)
XLA Ops:
  8.4 25.9 %shard_map.221 = (bf16[16,48,1664]{2,1,0:T(8,128)(2,1)S(1)}, bf16[197,768]{1,0:T(8,128)(2,1)S(1)}, bf16[197,768]{1,0:T(8,128)(2,1)S(1)}) custom-call(bf16[48,1664]{1,0:T(8,128)(2,1)S(1)} %concatenate.19.shard, bf16[197,768]{1,0:T(8,128)(2,1)S(1)} %copy-done.1, bf16[197,768]{1,0:T(8,128)(2,1)S(1)} %copy-done.10), custom_call_target="tpu_custom_call" | custom-call | tf_op jit(solution)/shard_map/pallas_call | solution.py:58
  36.2 4.1 %shard_map.222 = (bf16[2,197,1152]{2,1,0:T(8,128)(2,1)S(1)}, bf16[2,197,384]{2,1,0:T(8,128)(2,1)S(1)}, bf16[394,768]{1,0:T(8,128)(2,1)S(1)}) custom-call(bf16[2,197,768]{2,1,0:T(8,128)(2,1)S(1)} %fusion.34.normed, bf16[768,1664]{1,0:T(8,128)(2,1)S(1)} %bitcast.85), custom_call_target="tpu_custom_call" | custom-call | tf_op jit(solution)/shard_map/pallas_call | solution.py:442
  40.3 16.6 %shard_map.223 = bf16[394,768]{1,0:T(8,128)(2,1)S(1)} custom-call(bf16[394,768]{1,0:T(8,128)(2,1)S(1)} %get-tuple-element.28.refs_0_), custom_call_target="tpu_custom_call" | custom-call | tf_op jit(solution)/shard_map/pallas_call | solution.py:58
  59.8 2.2 maximum_convert_fusion
  62.0 2.0 convolution_convert_fusion
  66.0 46.8 %shard_map.224 = (bf16[16,64,768]{2,1,0:T(8,128)(2,1)S(1)}, bf16[16,64,768]{2,1,0:T(8,128)(2,1)S(1)}) custom-call(bf16[16,64,384]{2,1,0:T(8,128)(2,1)S(1)} %bitcast.98, bf16[16,64,384]{2,1,0:T(8,128)(2,1)S(1)} %bitcast.99), custom_call_target="tpu_custom_call" | custom-call | tf_op jit(solution)/shard_map/pallas_call | solution.py:58
  112.8 2.6 fusion.15
  115.5 4.2 %fusion.20 = bf16[1024,768]{1,0:T(8,128)(2,1)S(1)} fusion(bf16[1,1536,768]{2,1,0:T(8,128)(2,1)S(1)} %copy-done, f32[1024,1536]{1,0:T(8,128)S(1)} %fusion.15), kind=kOutput, calls=%fused_computation.22 | convolution fusion | flops 2430861312 | bytes 10223616 | tf_op jit(solution)/shard_map/dot_general | solution.py:581
  119.7 6.3 %fusion.6 = bf16[1024,1536]{1,0:T(8,128)(2,1)S(1)} fusion(f32[1024,1536]{1,0:T(8,128)S(1)} %fusion.15, bf16[1024,768]{1,0:T(8,128)(2,1)S(1)} %bitcast.100, bf16[1,1536,768]{2,1,0:T(8,128)(2,1)S(1)} %copy-done), kind=kOutput, calls=%fused_computation.8 | convolution fusion | flops 2447376384 | bytes 13369344 | tf_op jit(solution)/shard_map/dot_general | solution.py:582
  126.1 2.6 fusion.17
  128.7 48.7 %shard_map.225 = (bf16[16,64,384]{2,1,0:T(8,128)(2,1)S(1)}, bf16[16,64,384]{2,1,0:T(8,128)(2,1)S(1)}) custom-call(bf16[16,64,768]{2,1,0:T(8,128)(2,1)S(1)} %bitcast.96, bf16[16,64,768]{2,1,0:T(8,128)(2,1)S(1)} %bitcast.97), custom_call_target="tpu_custom_call" | custom-call | tf_op jit(solution)/shard_map/pallas_call | solution.py:58
  182.9 1.5 collective-permute-start
  184.4 4.3 %convolution_bitcast_fusion.1 = f32[1,768,1536]{2,1,0:T(8,128)} fusion(bf16[1024,768]{1,0:T(8,128)(2,1)S(1)} %bitcast.95, bf16[1024,1536]{1,0:T(8,128)(2,1)S(1)} %fusion.6), kind=kOutput, calls=%fused_computation.11 | convolution fusion | flops 2415919104 | bytes 9437184 | tf_op jit(solution)/shard_map/dot_general | solution.py:595
  188.9 14.9 %convolution_bitcast_fusion = f32[1,1536,768]{2,1,0:T(8,128)} fusion(bf16[1024,768]{1,0:T(8,128)(2,1)S(1)} %bitcast.101, f32[1024,1536]{1,0:T(8,128)S(1)} %bitcast.132), kind=kOutput, calls=%fused_computation.10 | convolution fusion | flops 2430074880 | bytes 12582912 | tf_op jit(solution)/shard_map/dot_general | solution.py:594
  203.9 2.8 fusion.37
  207.8 2.1 multiply_reduce_fusion
  211.0 1.5 fusion.76
  212.5 2.0 reshape.178.grad_branch
  217.9 12.4 %shard_map.226 = (bf16[768,1664]{1,0:T(8,128)(2,1)}, f32[2,197,768]{2,1,0:T(8,128)S(1)}) custom-call(bf16[2,197,768]{2,1,0:T(8,128)(2,1)S(1)} %copy-done.7, bf16[2,197,1152]{2,1,0:T(8,128)(2,1)S(1)} %copy-done.13, bf16[2,197,384]{2,1,0:T(8,128)(2,1)S(1)} %get-tuple-element.34.heads_out, bf16[2,197,768]{2,1,0:T(8,128)(2,1)S(1)} %copy-done.9, ...), custom_call_target="tpu_custom_call" | custom-call | tf_op jit(solution)/shard_map/pallas_call | solution.py:442
  233.7 2.2 concatenate.24
  235.8 1.6 constant_dynamic-update-slice_fusion
  237.5 1.7 copy-done.8
  239.2 32.1 %shard_map.227 = (f32[48,1664]{1,0:T(8,128)S(1)}, f32[48,128]{1,0:T(8,128)S(1)}, bf16[197,768]{1,0:T(8,128)(2,1)S(1)}) custom-call(bf16[16,48,1664]{2,1,0:T(8,128)(2,1)S(1)} %bitcast.93, bf16[197,768]{1,0:T(8,128)(2,1)S(1)} %fusion.56.rows), custom_call_target="tpu_custom_call" | custom-call | tf_op jit(solution)/shard_map/pallas_call | solution.py:58
  277.2 2.0 dynamic-slice_add_fusion.1
  (130 shorter events, 35.6 us)
Async XLA Ops:
  0.6 114.8 %copy-start = (bf16[1,1536,768]{2,1,0:T(8,128)(2,1)S(1)}, bf16[1,1536,768]{2,1,0:T(8,128)(2,1)}, u32[]{:S(2)}) copy-start(bf16[1,1536,768]{2,1,0:T(8,128)(2,1)} %param.23) | copy-start | bytes 7077892
  34.2 24.6 %copy-start.5 = (bf16[16,48,1664]{2,1,0:T(8,128)(2,1)}, bf16[16,48,1664]{2,1,0:T(8,128)(2,1)S(1)}, u32[]{:S(2)}) copy-start(bf16[16,48,1664]{2,1,0:T(8,128)(2,1)S(1)} %get-tuple-element.27) | copy-start | bytes 7667716
  36.1 4.2 %copy-start.6 = (bf16[2,197,768]{2,1,0:T(8,128)(2,1)}, bf16[2,197,768]{2,1,0:T(8,128)(2,1)S(1)}, u32[]{:S(2)}) copy-start(bf16[2,197,768]{2,1,0:T(8,128)(2,1)S(1)} %fusion.34.normed) | copy-start | bytes 1815556
  36.1 20.8 %copy-start.2 = (bf16[197,768]{1,0:T(8,128)(2,1)S(1)}, bf16[197,768]{1,0:T(8,128)(2,1)}, u32[]{:S(2)}) copy-start(bf16[197,768]{1,0:T(8,128)(2,1)} %rows_a.1) | copy-start | bytes 907780
  36.1 20.8 %copy-start.11 = (bf16[197,768]{1,0:T(8,128)(2,1)S(1)}, bf16[197,768]{1,0:T(8,128)(2,1)}, u32[]{:S(2)}) copy-start(bf16[197,768]{1,0:T(8,128)(2,1)} %rows_b.1) | copy-start | bytes 907780
  40.3 17.6 %copy-start.12 = (bf16[2,197,1152]{2,1,0:T(8,128)(2,1)}, bf16[2,197,1152]{2,1,0:T(8,128)(2,1)S(1)}, u32[]{:S(2)}) copy-start(bf16[2,197,1152]{2,1,0:T(8,128)(2,1)S(1)} %get-tuple-element.33.mixed) | copy-start | bytes 2723332
  58.5 1.2 copy-start.23
  58.5 1.2 copy-start.22
  58.5 1.3 copy-start.24
  62.0 2.0 copy-start.21
  65.0 47.8 %copy-start.25 = (bf16[1,768,1536]{2,1,0:T(8,128)(2,1)S(1)}, bf16[1,768,1536]{2,1,0:T(8,128)(2,1)}, u32[]{:S(2)}) copy-start(bf16[1,768,1536]{2,1,0:T(8,128)(2,1)} %param.22) | copy-start | bytes 7077892
  115.5 4.2 %copy-start.27 = (f32[1024,1536]{1,0:T(8,128)}, f32[1024,1536]{1,0:T(8,128)S(1)}, u32[]{:S(2)}) copy-start(f32[1024,1536]{1,0:T(8,128)S(1)} %fusion.15) | copy-start | bytes 18874372
  119.7 6.4 %copy-start.26 = (bf16[1,768,1536]{2,1,0:T(8,128)(2,1)S(1)}, bf16[1,768,1536]{2,1,0:T(8,128)(2,1)}, u32[]{:S(2)}) copy-start(bf16[1,768,1536]{2,1,0:T(8,128)(2,1)} %param.22) | copy-start | bytes 7077892
  178.7 27.9 %collective-permute-start.1 = (bf16[394,384]{1,0:T(8,128)(2,1)}, bf16[394,384]{1,0:T(8,128)(2,1)}, u32[]{:S(2)}, u32[]{:S(2)}) collective-permute-start(bf16[394,384]{1,0:T(8,128)(2,1)} %convolution_convert_fusion.1), channel_id=1, source_target_pairs={{0,1},{1,0},{2,3},{3,2},{4,5},{5,4},{6,7},{7,6},{8,9},{9,8},{10,11... | collective-permute-start | bytes 907784 | tf_op jit(solution)/shard_map/ppermute | solution.py:605
  180.8 8.0 %slice-start = ((s8[6291456]{0:T(1024)(128)(4,1)}), s8[4194304]{0:T(1024)(128)(4,1)S(1)}, s32[]{:S(2)}) async-start(s8[6291456]{0:T(1024)(128)(4,1)} %bitcast.131), calls=%async_computation | async-start | bytes 8388608
  182.3 21.5 %collective-permute-start.2 = (f32[2,394]{1,0:T(2,128)S(1)}, f32[2,394]{1,0:T(2,128)S(1)}, u32[]{:S(2)}, u32[]{:S(2)}) collective-permute-start(f32[2,394]{1,0:T(2,128)S(1)} %pad_maximum_fusion), channel_id=1, source_target_pairs={{0,1},{1,0},{2,3},{3,2},{4,5},{5,4},{6,7},{7,6},{8,9},{9,8},{10,11... | collective-permute-start | bytes 9464 | tf_op jit(solution)/shard_map/ppermute | solution.py:606
  182.9 5.9 %slice-start.1 = ((s8[6291456]{0:T(1024)(128)(4,1)}), s8[2097152]{0:T(1024)(128)(4,1)S(1)}, s32[]{:S(2)}) async-start(s8[6291456]{0:T(1024)(128)(4,1)} %bitcast.131), calls=%async_computation.1 | async-start | bytes 4194304
  182.9 91.9 %collective-permute-start = (bf16[394,384]{1,0:T(8,128)(2,1)}, bf16[394,384]{1,0:T(8,128)(2,1)}, u32[]{:S(2)}, u32[]{:S(2)}) collective-permute-start(bf16[394,384]{1,0:T(8,128)(2,1)} %get-tuple-element.112), channel_id=1, source_target_pairs={{0,1},{1,0},{2,3},{3,2},{4,5},{5,4},{6,7},{7,6},{8,9},{9,8},{10,11... | collective-permute-start | bytes 907784 | tf_op jit(solution)/shard_map/ppermute | solution.py:604
  203.8 4.0 %copy-start.15 = (f32[394,768]{1,0:T(8,128)S(1)}, f32[394,768]{1,0:T(8,128)}, u32[]{:S(2)}) copy-start(f32[394,768]{1,0:T(8,128)} %copy-done.14) | copy-start | bytes 3631108
  216.7 1.2 copy-start.13
  237.5 1.7 copy-start.8
  239.2 33.5 %copy-start.4 = (f32[2,197,768]{2,1,0:T(8,128)S(1)}, f32[2,197,768]{2,1,0:T(8,128)}, u32[]{:S(2)}) copy-start(f32[2,197,768]{2,1,0:T(8,128)} %copy-done.3) | copy-start | bytes 3631108
  274.8 1.5 copy-start.16
  274.8 2.4 copy-start.18
  (9 other events, 9.1 us)
